TPU v7x, 32 devices: a whole 2x2x4 slice. The times are simulated.
32 devices in a mesh: clips: 2 (over y), seq: 4 (over z), cache: 2 (over x), head: 2 (over core).
Axes of the slice: x: 2, y: 2, z: 4, core: 2. Of those that a mesh axis runs over, the one named last changes fastest.
Arguments:
- queries: bfloat16 [3072, 6144], P(('clips', 'seq'), ('cache', 'head')), parts along dimension 0, may hold values from -5 to 5
- keys: bfloat16 [3072, 6144], P(('clips', 'seq'), ('cache', 'head')), parts along dimension 0, may hold values from -5 to 5
- values: bfloat16 [3072, 6144], P(('clips', 'seq'), ('cache', 'head')), parts along dimension 0, may hold values from -6 to 6
- frame_ids: int32 [3072], P(('clips', 'seq')), parts along dimension 0, may hold values from 0 to 7, never falling along the last dimension, each value on 1 to 384 neighbouring positions
- past_keys: bfloat16 [32, 64, 6144], P(('clips', 'seq'), None, ('cache', 'head')), parts along dimension 0, may hold values from -6 to 6
- past_values: bfloat16 [32, 64, 6144], P(('clips', 'seq'), None, ('cache', 'head')), parts along dimension 0, may hold values from -6 to 6
- block_home: int32 [32], P('clips'), parts along dimension 0, may hold values from 0 to 15, as said below
- windows: int32 [8, 4], P('clips'), parts along dimension 0, may hold values from 0 to 15, as said below
- window_len: int32 [8], P('clips'), parts along dimension 0, may hold values from 3 to 4, as said below
Outputs:
- attended: bfloat16 [3072, 6144], P(('clips', 'seq'), ('cache', 'head')), parts along dimension 0
There are 2 independent parts, one for each index of `clips`. A program takes and returns all parts, laid end to end along the dimension named above; each array names one. Nothing has to cross between parts.
Inputs may be any that keep to these rules, and one draw needn't show every extreme that they name: `block_home`: a random order of the 16 storage rows. `windows`: each row holds 4 different past blocks; among the live ones of a row at most 2 have block_home in one owner's range owner * 4 to owner * 4 + 3, and some row reaches 2. `window_len`: some shard has all 4 entries live.
All inputs are finite; a program needn't handle non-finite values.
Results may differ from a plain program's by a relative error of at most 0.006.
Values may be sent and summed in bfloat16 or wider, within the bound.
A program may use at most 64 MiB of HBM per device.

v0:
```python
import math

import jax
import jax.numpy as jnp
from jax import lax
from jax.sharding import PartitionSpec as P

HEAD_DIM = 128


masked_score = -1e30


def shifted(block, axis, distance):
    devices = range(lax.axis_size(axis))
    route = [((i - distance) % len(devices), i) for i in devices]
    return lax.ppermute(block, axis, route)


def on_device(
    queries, keys, values, frame_ids, past_keys, past_values, block_home, windows, window_len
):
    row_count = queries.shape[0]
    feature_width = queries.shape[1]
    head_count = feature_width // HEAD_DIM
    seq_count = lax.axis_size("seq")
    my_index = lax.axis_index("seq")
    score_scale = HEAD_DIM ** (-0.5)
    query_heads = queries.reshape(row_count, head_count, HEAD_DIM)

    def attend(carried, key_rows, value_rows, key_mask):
        run_max, run_sum, run_acc = carried
        scores = (
            jnp.einsum("qhd,khd->hqk", query_heads, key_rows, preferred_element_type=jnp.float32)
            * score_scale
        )
        scores = jnp.where(key_mask[None], scores, masked_score)
        new_max = jnp.maximum(run_max, jnp.max(scores, axis=-1))
        weights = jnp.where(key_mask[None], jnp.exp(scores - new_max[..., None]), 0.0)
        rescale = jnp.exp(run_max - new_max)
        run_sum = run_sum * rescale + jnp.sum(weights, axis=-1)
        update = jnp.einsum(
            "hqk,khd->qhd",
            weights.astype(jnp.bfloat16),
            value_rows,
            preferred_element_type=jnp.float32,
        )
        run_acc = run_acc * rescale.T[..., None] + update
        return (new_max, run_sum, run_acc)

    carried = (
        jnp.full((head_count, row_count), masked_score, jnp.float32),
        jnp.zeros((head_count, row_count), jnp.float32),
        jnp.zeros((row_count, head_count, HEAD_DIM), jnp.float32),
    )
    every_frame = lax.all_gather(frame_ids, "seq", axis=0, tiled=True)
    self_mask = frame_ids[None, :] <= frame_ids[:, None]
    carried = attend(
        carried,
        keys.reshape(row_count, head_count, HEAD_DIM),
        values.reshape(row_count, head_count, HEAD_DIM),
        self_mask,
    )

    def cycle_body(offset, loop_state):
        moving, running = loop_state
        moving = shifted(moving, "seq", 1)
        source = (my_index - offset) % seq_count
        key_frames = lax.dynamic_slice_in_dim(every_frame, source * row_count, row_count, 0)
        key_mask = key_frames[None, :] <= frame_ids[:, None]
        key_rows = moving[0].reshape(row_count, head_count, HEAD_DIM)
        value_rows = moving[1].reshape(row_count, head_count, HEAD_DIM)
        running = attend(running, key_rows, value_rows, key_mask)
        return (moving, running)

    moving = jnp.stack([keys, values])
    moving, carried = lax.fori_loop(1, seq_count, cycle_body, (moving, carried))
    list_len = windows.shape[1]
    block_len = past_keys.shape[1]
    my_rows = block_home[lax.dynamic_index_in_dim(windows, my_index, 0, keepdims=False)]
    my_len = lax.dynamic_index_in_dim(window_len, my_index, 0, keepdims=False)
    live_slots = jnp.arange(list_len) < my_len
    running = carried
    piece_keys = lax.all_gather(past_keys, "seq", axis=0, tiled=True)
    piece_values = lax.all_gather(past_values, "seq", axis=0, tiled=True)
    block_count = piece_keys.shape[0]
    grouping = math.gcd(block_count, 8)
    row_ids = jnp.arange(block_count)
    member = jnp.any((row_ids[:, None] == my_rows[None, :]) & live_slots[None, :], axis=1)
    group_keys = piece_keys.reshape(
        block_count // grouping, grouping * block_len, head_count, HEAD_DIM
    )
    group_values = piece_values.reshape(
        block_count // grouping, grouping * block_len, head_count, HEAD_DIM
    )
    group_mask = jnp.repeat(member.reshape(block_count // grouping, grouping), block_len, axis=1)

    def one_group(inside, items):
        item_keys, item_values, item_mask = items
        full_mask = jnp.broadcast_to(item_mask[None, :], (row_count, item_mask.shape[0]))
        return (attend(inside, item_keys, item_values, full_mask), None)

    running, unused = lax.scan(one_group, running, (group_keys, group_values, group_mask))
    carried = running
    run_max, run_sum, run_acc = carried
    output = run_acc / run_sum.T[..., None]
    return output.reshape(row_count, feature_width).astype(jnp.bfloat16)


def solution(mesh):
    in_specs = (
        P(("clips", "seq"), ("cache", "head")),
        P(("clips", "seq"), ("cache", "head")),
        P(("clips", "seq"), ("cache", "head")),
        P(("clips", "seq")),
        P(("clips", "seq"), None, ("cache", "head")),
        P(("clips", "seq"), None, ("cache", "head")),
        P("clips"),
        P("clips", None),
        P("clips"),
    )
    out_specs = P(("clips", "seq"), ("cache", "head"))
    return jax.shard_map(
        on_device, mesh=mesh, in_specs=in_specs, out_specs=out_specs, check_vma=False
    )
```

profile of v0, /device:TPU:0, one launch (start us, length us, event | category | flops | bytes accessed | tf_op | source)
XLA Modules:
  0.0 368.1 jit_solution(10176256946042532781)
XLA Ops:
  8.0 1.6 broadcast_compare_fusion.1
  10.3 1.7 copy.61
  12.7 0.8 copy.68
  13.5 2.4 fusion.37
  16.6 2.5 fusion.39
  19.7 1.7 copy.60
  21.4 13.9 %all-gather = s32[4,1,384]{2,1,0:T(1,128)S(1)} all-gather(s32[1,1,384]{2,1,0:T(1,128)S(1)} %reshape.137), channel_id=1, replica_groups=mesh['clips'=2,'seq'=4,'cache'=2,'head'=2] {'seq'}, dimensions={0}, use_global_device_ids=true | all-gather | bytes 7680 | tf_op jit(solution)/shard_map/all_gather | solution.py:56
  36.6 7.2 %bitcast_add_fusion.2 = f32[384,12,128]{2,0,1:T(8,128)} fusion(bf16[384,12,128]{0,2,1:T(8,128)(2,1)S(1)} %bitcast.92, f32[12,384,384]{1,2,0:T(8,128)} %copy-done.2, f32[12,384]{1,0:T(8,128)} %broadcast_maximum_fusion, pred[384,384]{0,1:T(8,128)(4,1)} %broadcast_compare_fusion.1, f32[384,12]{0,1:T(8,128)} %get-tuple-element.379), kind=kOutput, calls=%fused_computation.57 | convolution fusion | flops 462422016 | bytes 10801152 | tf_op jit(solution)/shard_map/hqk,khd->qhd/dot_general | solution.py:42
  43.8 1.7 pad_maximum_fusion
  45.5 258.9 %while.35 = (s32[]{:T(128)}, bf16[2,384,1536]{1,2,0:T(8,128)(2,1)}, f32[12,384]{1,0:T(8,128)}, f32[12,384]{1,0:T(8,128)}, f32[384,12,128]{2,0,1:T(8,128)}, /*ind...) while((s32[]{:T(128)}, bf16[2,384,1536]{1,2,0:T(8,128)(2,1)}, ...), condition=%wide.region_5.6_spmd, body=%wide.region_2.5_spmd.sunk | while | flops 930313728 | bytes 68131224 | solution.py:77
  45.5 1.5 collective-permute-start
  47.2 91.3 %collective-permute-done = bf16[2,384,1536]{1,2,0:T(8,128)(2,1)S(1)} collective-permute-done((bf16[2,384,1536]{1,2,0:T(8,128)(2,1)}, bf16[2,384,1536]{1,2,0:T(8,128)(2,1)S(1)}, u32[]{:S(2)}, u32[]{:S(2)}) %collective-permute-start) | collective-permute-done | bytes 2359328 | tf_op jit(solution)/shard_map/while/body/eval_jaxpr/ppermute | solution.py:17
  138.8 1.4 fusion.83
  140.9 1.7 fusion.85
  142.6 1.4 multiply_add_fusion.4
  144.6 3.0 bitcast_add_fusion.5
  147.7 1.5 copy.93
  149.8 9.5 %collective-permute-start = (bf16[2,384,1536]{1,2,0:T(8,128)(2,1)}, bf16[2,384,1536]{1,2,0:T(8,128)(2,1)S(1)}, u32[]{:S(2)}, u32[]{:S(2)}) collective-permute-start(bf16[2,384,1536]{1,2,0:T(8,128)(2,1)} %get-tuple-element.523), channel_id=1, source_target_pairs={{12,0},{0,4},{4,8},{8,12},{13,1},{1,5},{5,9},{9,13},{14,2},{2,6},{... | collective-permute-start | bytes 7077896 | tf_op jit(solution)/shard_map/while/body/eval_jaxpr/ppermute | solution.py:17
  159.6 67.5 %collective-permute-done = bf16[2,384,1536]{1,2,0:T(8,128)(2,1)S(1)} collective-permute-done((bf16[2,384,1536]{1,2,0:T(8,128)(2,1)}, bf16[2,384,1536]{1,2,0:T(8,128)(2,1)S(1)}, u32[]{:S(2)}, u32[]{:S(2)}) %collective-permute-start) | collective-permute-done | bytes 2359328 | tf_op jit(solution)/shard_map/while/body/eval_jaxpr/ppermute | solution.py:17
  227.3 1.4 fusion.83
  229.4 1.7 fusion.85
  231.1 1.4 multiply_add_fusion.4
  233.1 3.0 bitcast_add_fusion.5
  236.2 1.5 copy.93
  238.6 54.5 %collective-permute-done = bf16[2,384,1536]{1,2,0:T(8,128)(2,1)S(1)} collective-permute-done((bf16[2,384,1536]{1,2,0:T(8,128)(2,1)}, bf16[2,384,1536]{1,2,0:T(8,128)(2,1)S(1)}, u32[]{:S(2)}, u32[]{:S(2)}) %collective-permute-start) | collective-permute-done | bytes 2359328 | tf_op jit(solution)/shard_map/while/body/eval_jaxpr/ppermute | solution.py:17
  293.3 1.4 fusion.83
  295.5 1.7 fusion.85
  297.2 1.4 multiply_add_fusion.4
  299.2 3.0 bitcast_add_fusion.5
  302.2 1.5 copy.93
  304.4 2.0 copy.69
  309.4 6.9 %reshape.127 = bf16[2,512,12,128]{3,2,1,0:T(8,128)(2,1)} reshape(bf16[16,64,1536]{2,1,0:T(8,128)(2,1)} %all-gather.4.cloned.1.call-done) | data formatting | bytes 6291456 | tf_op jit(solution)/shard_map/reshape | solution.py:90
  316.2 4.7 %copy.70 = bf16[2,512,12,128]{3,1,2,0:T(8,128)(2,1)} copy(bf16[2,512,12,128]{3,2,1,0:T(8,128)(2,1)} %reshape.127) | data formatting | bytes 6291456 | tf_op jit(solution)/shard_map/while | solution.py:103
  321.0 6.9 %reshape.128 = bf16[2,512,12,128]{3,2,1,0:T(8,128)(2,1)} reshape(bf16[16,64,1536]{2,1,0:T(8,128)(2,1)} %all-gather.6.cloned.1.call-done) | data formatting | bytes 6291456 | tf_op jit(solution)/shard_map/reshape | solution.py:93
  327.8 7.5 %copy.72 = bf16[2,512,12,128]{1,3,2,0:T(8,128)(2,1)} copy(bf16[2,512,12,128]{3,2,1,0:T(8,128)(2,1)} %reshape.128) | data formatting | bytes 6291456 | tf_op jit(solution)/shard_map/while | solution.py:103
  335.3 23.5 %while.36 = (s32[]{:T(128)}, f32[12,384]{1,0:T(8,128)}, f32[12,384]{1,0:T(8,128)}, f32[384,12,128]{0,2,1:T(8,128)S(1)}, pred[2,512]{1,0:T(4,128)(4,1)S(1)}, /*in...) while((s32[]{:T(128)}, f32[12,384]{1,0:T(8,128)}, ...), condition=%wide.region_10.11_spmd, body=%wide.region_7.10_spmd.sunk | while | flops 1239823872 | bytes 50249344 | solution.py:103
  335.3 3.1 bitcast_reduce_fusion.2
  338.5 0.8 fusion.89
  339.2 3.2 bitcast_add_fusion.6
  342.4 2.7 fusion.90
  345.1 1.4 multiply_add_fusion.5
  347.1 3.1 bitcast_reduce_fusion.2
  350.3 0.8 fusion.89
  351.0 3.2 bitcast_add_fusion.6
  354.2 2.7 fusion.90
  356.9 1.4 multiply_add_fusion.5
  358.8 1.0 divide_convert_fusion
  359.8 1.5 copy.73
  (71 shorter events, 17.2 us)
Async XLA Ops:
  6.5 301.2 %copy-start = (s32[16]{0:T(128)S(1)}, s32[16]{0:T(128)}, u32[]{:S(2)}) copy-start(s32[16]{0:T(128)} %param.19) | copy-start | bytes 196
  6.5 5.4 %copy-start.7 = (bf16[384,1536]{1,0:T(8,128)(2,1)S(1)}, bf16[384,1536]{1,0:T(8,128)(2,1)}, u32[]{:S(2)}) copy-start(bf16[384,1536]{1,0:T(8,128)(2,1)} %param.14) | copy-start | bytes 3538948
  6.5 302.8 %all-gather.4.cloned.1.call-start = ((), (), s32[]{:S(2)}) async-start(), calls=%async_computation | async-start | bytes 3932160 | tf_op jit(solution)/shard_map/all_gather | solution.py:84
  7.3 313.7 %all-gather.6.cloned.1.call-start = ((), (), s32[]{:S(2)}) async-start(), calls=%async_computation.1 | async-start | bytes 3932160 | tf_op jit(solution)/shard_map/all_gather | solution.py:85
  13.5 3.1 copy-start.6
  15.9 3.1 copy-start.2
  43.8 1.7 copy-start.8
  45.5 93.1 %collective-permute-start = (bf16[2,384,1536]{1,2,0:T(8,128)(2,1)}, bf16[2,384,1536]{1,2,0:T(8,128)(2,1)S(1)}, u32[]{:S(2)}, u32[]{:S(2)}) collective-permute-start(bf16[2,384,1536]{1,2,0:T(8,128)(2,1)} %get-tuple-element.523), channel_id=1, source_target_pairs={{12,0},{0,4},{4,8},{8,12},{13,1},{1,5},{5,9},{9,13},{14,2},{2,6},{... | collective-permute-start | bytes 7077896 | tf_op jit(solution)/shard_map/while/body/eval_jaxpr/ppermute | solution.py:17
  140.9 3.7 %copy-start.4 = (f32[384,12,128]{2,0,1:T(8,128)S(1)}, f32[384,12,128]{2,0,1:T(8,128)}, u32[]{:S(2)}) copy-start(f32[384,12,128]{2,0,1:T(8,128)} %get-tuple-element.526) | copy-start | bytes 7077892 | tf_op jit(solution)/shard_map/while
  147.7 2.2 copy-start.5
  149.8 77.2 %collective-permute-start = (bf16[2,384,1536]{1,2,0:T(8,128)(2,1)}, bf16[2,384,1536]{1,2,0:T(8,128)(2,1)S(1)}, u32[]{:S(2)}, u32[]{:S(2)}) collective-permute-start(bf16[2,384,1536]{1,2,0:T(8,128)(2,1)} %get-tuple-element.523), channel_id=1, source_target_pairs={{12,0},{0,4},{4,8},{8,12},{13,1},{1,5},{5,9},{9,13},{14,2},{2,6},{... | collective-permute-start | bytes 7077896 | tf_op jit(solution)/shard_map/while/body/eval_jaxpr/ppermute | solution.py:17
  229.4 3.7 %copy-start.4 = (f32[384,12,128]{2,0,1:T(8,128)S(1)}, f32[384,12,128]{2,0,1:T(8,128)}, u32[]{:S(2)}) copy-start(f32[384,12,128]{2,0,1:T(8,128)} %get-tuple-element.526) | copy-start | bytes 7077892 | tf_op jit(solution)/shard_map/while
  236.1 2.2 copy-start.5
  238.3 54.8 %collective-permute-start = (bf16[2,384,1536]{1,2,0:T(8,128)(2,1)}, bf16[2,384,1536]{1,2,0:T(8,128)(2,1)S(1)}, u32[]{:S(2)}, u32[]{:S(2)}) collective-permute-start(bf16[2,384,1536]{1,2,0:T(8,128)(2,1)} %get-tuple-element.523), channel_id=1, source_target_pairs={{12,0},{0,4},{4,8},{8,12},{13,1},{1,5},{5,9},{9,13},{14,2},{2,6},{... | collective-permute-start | bytes 7077896 | tf_op jit(solution)/shard_map/while/body/eval_jaxpr/ppermute | solution.py:17
  295.5 3.7 %copy-start.4 = (f32[384,12,128]{2,0,1:T(8,128)S(1)}, f32[384,12,128]{2,0,1:T(8,128)}, u32[]{:S(2)}) copy-start(f32[384,12,128]{2,0,1:T(8,128)} %get-tuple-element.526) | copy-start | bytes 7077892 | tf_op jit(solution)/shard_map/while
  302.2 2.2 copy-start.5
  304.4 2.1 copy-start.9
  335.3 3.9 %copy-start.3 = (bf16[2,512,12,128]{1,3,2,0:T(8,128)(2,1)S(1)}, bf16[2,512,12,128]{1,3,2,0:T(8,128)(2,1)}, u32[]{:S(2)}) copy-start(bf16[2,512,12,128]{1,3,2,0:T(8,128)(2,1)} %get-tuple-element.577) | copy-start | bytes 9437188 | tf_op jit(solution)/shard_map/while
  347.1 3.9 %copy-start.3 = (bf16[2,512,12,128]{1,3,2,0:T(8,128)(2,1)S(1)}, bf16[2,512,12,128]{1,3,2,0:T(8,128)(2,1)}, u32[]{:S(2)}) copy-start(bf16[2,512,12,128]{1,3,2,0:T(8,128)(2,1)} %get-tuple-element.577) | copy-start | bytes 9437188 | tf_op jit(solution)/shard_map/while
  358.8 2.5 copy-start.1
Sparse Core Ops, SparseCore 0:
  8.9 91.1 all-gather.3
  101.7 90.3 all-gather.5
where the time goes:
time: 370 us; the launch traced here: 368 us
  waiting for transfers between devices  215 us (58%)
  local copies, waits for them, and re-layouts  47.7 us (13%)
  matrix products  35.4 us (10%)
  other arithmetic  31.6 us (9%)
  blocking collectives  13.9 us (4%)
  between operations  13.5 us (4%)
  starting transfers between devices  11.1 us (3%)
    ppermute x3, waiting for transfers between devices, shifted(): return lax.ppermute(block, axis, route)  213 us
    dot_general x6, matrix products, attend(): jnp.einsum('hqk,khd->qhd', weights.astype(jnp.bfloat16), value_rows, pref...  22.5 us
    while x3, local copies, waits for them, and re-layouts, on_device(): lax.scan(one_group, running, (group_keys, group_values, group_mask))  14.2 us
    all_gather x1, blocking collectives, on_device(): every_frame = lax.all_gather(frame_ids, 'seq', axis=0, tiled=True)  13.9 us
    reduce_sum x6, other arithmetic, attend(): run_sum = run_sum * rescale + jnp.sum(weights, axis=-1)  12.9 us
    dot_general x6, matrix products, attend(): jnp.einsum('qhd,khd->hqk', query_heads, key_rows, preferred_element_type=...  12.8 us
    ppermute x3, starting transfers between devices, shifted(): return lax.ppermute(block, axis, route)  11.1 us
    while x24, local copies, waits for them, and re-layouts  9.52 us
  transfers between devices with their start and end apart: 5, of which 3 were waited for; matrix products, arithmetic and copies ran while one was open for 20% of the time, Pallas kernels for 0%

commit v1 on v0

--- a/solution.py
+++ b/solution.py
@@ -1,8 +1,11 @@
+import functools
 import math
 
 import jax
 import jax.numpy as jnp
 from jax import lax
+from jax.experimental import pallas as pl
+from jax.experimental.pallas import tpu as pltpu
 from jax.sharding import PartitionSpec as P
 
 HEAD_DIM = 128
@@ -106,6 +109,259 @@
     output = run_acc / run_sum.T[..., None]
     return output.reshape(row_count, feature_width).astype(jnp.bfloat16)
 
+MESH = pl.DeviceIdType.MESH
+LOG2E = 1.4426950408889634
+
+
+def dot_nt(a, b):
+    return lax.dot_general(a, b, (((1,), (1,)), ((), ())), preferred_element_type=jnp.float32)
+
+
+def dot_tn(a, b):
+    return lax.dot_general(a, b, (((0,), (0,)), ((), ())), preferred_element_type=jnp.float32)
+
+
+def heads_kernel(
+    n,
+    q_ref,
+    k_ref,
+    v_ref,
+    frames_ref,
+    pk_ref,
+    pv_ref,
+    home_ref,
+    windows_ref,
+    len_ref,
+    out_ref,
+    qb,
+    kb,
+    vb,
+    fb,
+    frame_col,
+    pkb,
+    pvb,
+    past_k,
+    past_v,
+    ob,
+    send_sem,
+    recv_sem,
+    own_sem,
+    frame_send,
+    frame_recv,
+    out_send,
+    out_recv,
+    out_own,
+):
+    me = lax.axis_index("seq")
+    rows = q_ref.shape[0]
+    heads_here = qb.shape[0]
+    width = heads_here * HEAD_DIM
+    blocks = pk_ref.shape[0]
+    blk = pk_ref.shape[1]
+    win = windows_ref.shape[1]
+    scale = LOG2E * HEAD_DIM ** (-0.5)
+
+    barrier = pltpu.get_barrier_semaphore()
+    for t in range(1, n):
+        pl.semaphore_signal(
+            barrier, inc=1, device_id={"seq": lax.rem(me + t, n)}, device_id_type=MESH
+        )
+    pl.semaphore_wait(barrier, n - 1)
+
+    def pairs(h, dest, source):
+        columns = pl.ds(pl.multiple_of(dest * width + h * HEAD_DIM, HEAD_DIM), HEAD_DIM)
+        span = pl.ds(source * blocks, blocks)
+        return [
+            (q_ref.at[:, columns], qb.at[h, source]),
+            (k_ref.at[:, columns], kb.at[h, source]),
+            (v_ref.at[:, columns], vb.at[h, source]),
+            (pk_ref.at[:, :, columns], pkb.at[h, span]),
+            (pv_ref.at[:, :, columns], pvb.at[h, span]),
+        ]
+
+    def sends(h):
+        made = []
+        for t in range(1, n):
+            dest = lax.rem(me + t, n)
+            for i, (src, dst) in enumerate(pairs(h, dest, me)):
+                made.append(
+                    pltpu.make_async_remote_copy(
+                        src_ref=src,
+                        dst_ref=dst,
+                        send_sem=send_sem.at[h, t, i],
+                        recv_sem=recv_sem.at[h, t, i],
+                        device_id={"seq": dest},
+                        device_id_type=MESH,
+                    )
+                )
+        return made
+
+    def owns(h):
+        return [
+            pltpu.make_async_copy(src, dst, own_sem.at[h, i])
+            for i, (src, dst) in enumerate(pairs(h, me, me))
+        ]
+
+    def frame_send_of(t):
+        return pltpu.make_async_remote_copy(
+            src_ref=frames_ref,
+            dst_ref=fb.at[me],
+            send_sem=frame_send.at[t],
+            recv_sem=frame_recv.at[t],
+            device_id={"seq": lax.rem(me + t, n)},
+            device_id_type=MESH,
+        )
+
+    def start(h):
+        for copy in sends(h):
+            copy.start()
+        for copy in owns(h):
+            copy.start()
+
+    for t in range(1, n):
+        frame_send_of(t).start()
+    start(0)
+    if heads_here > 1:
+        start(1)
+    fb[me] = frames_ref[...]
+    for t in range(1, n):
+        frame_send_of(t).wait()
+    for s in range(n):
+        frame_col[s] = jnp.transpose(fb[s])
+
+    def out_copy(h, t):
+        dest = lax.rem(me + t, n)
+        columns = pl.ds(pl.multiple_of(me * width + h * HEAD_DIM, HEAD_DIM), HEAD_DIM)
+        return pltpu.make_async_remote_copy(
+            src_ref=ob.at[h, dest],
+            dst_ref=out_ref.at[:, columns],
+            send_sem=out_send.at[h, t],
+            recv_sem=out_recv.at[h, t],
+            device_id={"seq": dest},
+            device_id_type=MESH,
+        )
+
+    def out_own_copy(h):
+        columns = pl.ds(pl.multiple_of(me * width + h * HEAD_DIM, HEAD_DIM), HEAD_DIM)
+        return pltpu.make_async_copy(ob.at[h, me], out_ref.at[:, columns], out_own.at[h])
+
+    def one_head(h, carry):
+        for copy in sends(h):
+            copy.wait_recv()
+        for copy in owns(h):
+            copy.wait()
+
+        @pl.when(h + 2 < heads_here)
+        def _():
+            start(h + 2)
+
+        past_k[...] = pkb[h]
+        past_v[...] = pvb[h]
+        for s in range(n):
+            query = qb[h, s]
+            state = (
+                jnp.full((1, rows), -1e30, jnp.float32),
+                jnp.zeros((1, rows), jnp.float32),
+                jnp.zeros((HEAD_DIM, rows), jnp.float32),
+            )
+
+            def update(state, key, value, allowed):
+                top, total, acc = state
+                score = dot_nt(key, query) * scale
+                if allowed is not None:
+                    score = jnp.where(allowed, score, -1e30)
+                new_top = jnp.maximum(top, jnp.max(score, axis=0, keepdims=True))
+                weight = jnp.exp2(score - new_top)
+                fade = jnp.exp2(top - new_top)
+                total = total * fade + jnp.sum(weight, axis=0, keepdims=True)
+                acc = acc * fade + dot_tn(value, weight.astype(jnp.bfloat16))
+                return new_top, total, acc
+
+            query_frame = fb[s, 0:1, :]
+            for j in range(min(s + 2, n)):
+                allowed = None
+                if j >= s:
+                    allowed = frame_col[j][:, 0:1] <= query_frame
+                state = update(state, kb[h, j], vb[h, j], allowed)
+            keys, values, live = [], [], []
+            for w in range(win):
+                row = home_ref[windows_ref[s, w]]
+                keys.append(past_k[row])
+                values.append(past_v[row])
+            slot = lax.broadcasted_iota(jnp.int32, (win * blk, 1), 0) // blk
+            live = slot < len_ref[s]
+            top, total, acc = update(
+                state, jnp.concatenate(keys, axis=0), jnp.concatenate(values, axis=0), live
+            )
+            ob[h, s] = jnp.transpose(acc / total).astype(jnp.bfloat16)
+        for t in range(1, n):
+            out_copy(h, t).start()
+        out_own_copy(h).start()
+        return carry
+
+    lax.fori_loop(0, heads_here, one_head, 0)
+
+    def finish(h, carry):
+        for copy in sends(h):
+            copy.wait_send()
+        for t in range(1, n):
+            out_copy(h, t).wait()
+        out_own_copy(h).wait()
+        return carry
+
+    lax.fori_loop(0, heads_here, finish, 0)
+
+
+def by_heads(
+    queries, keys, values, frame_ids, past_keys, past_values, block_home, windows, window_len
+):
+    n = lax.axis_size("seq")
+    rows, features = queries.shape
+    heads_here = features // HEAD_DIM // n
+    blocks, blk = past_keys.shape[0], past_keys.shape[1]
+    frames = jnp.broadcast_to(frame_ids[None, :].astype(jnp.float32), (8, rows))
+    anywhere = pl.BlockSpec(memory_space=pl.ANY)
+    vmem = pl.BlockSpec(memory_space=pltpu.VMEM)
+    smem = pl.BlockSpec(memory_space=pltpu.SMEM)
+    dma = pltpu.SemaphoreType.DMA
+    bf16 = jnp.bfloat16
+    return pl.pallas_call(
+        functools.partial(heads_kernel, n),
+        out_shape=jax.ShapeDtypeStruct((rows, features), bf16),
+        in_specs=[anywhere] * 3 + [vmem] + [anywhere] * 2 + [smem] * 3,
+        out_specs=anywhere,
+        scratch_shapes=[
+            pltpu.VMEM((heads_here, n, rows, HEAD_DIM), bf16),
+            pltpu.VMEM((heads_here, n, rows, HEAD_DIM), bf16),
+            pltpu.VMEM((heads_here, n, rows, HEAD_DIM), bf16),
+            pltpu.VMEM((n, 8, rows), jnp.float32),
+            pltpu.VMEM((n, rows, 8), jnp.float32),
+            pltpu.VMEM((heads_here, n * blocks, blk, HEAD_DIM), bf16),
+            pltpu.VMEM((heads_here, n * blocks, blk, HEAD_DIM), bf16),
+            pltpu.VMEM((n * blocks, blk, HEAD_DIM), bf16),
+            pltpu.VMEM((n * blocks, blk, HEAD_DIM), bf16),
+            pltpu.VMEM((heads_here, n, rows, HEAD_DIM), bf16),
+            dma((heads_here, n, 5)),
+            dma((heads_here, n, 5)),
+            dma((heads_here, 5)),
+            dma((n,)),
+            dma((n,)),
+            dma((heads_here, n)),
+            dma((heads_here, n)),
+            dma((heads_here,)),
+        ],
+        compiler_params=pltpu.CompilerParams(
+            collective_id=0, has_side_effects=True, vmem_limit_bytes=48 * 1024 * 1024
+        ),
+    )(queries, keys, values, frames, past_keys, past_values, block_home, windows, window_len)
+
+
+def pick(queries, *rest):
+    heads = queries.shape[1] // HEAD_DIM
+    if heads % lax.axis_size("seq") == 0:
+        return by_heads(queries, *rest)
+    return on_device(queries, *rest)
+
 
 def solution(mesh):
     in_specs = (
@@ -121,5 +377,5 @@
     )
     out_specs = P(("clips", "seq"), ("cache", "head"))
     return jax.shard_map(
-        on_device, mesh=mesh, in_specs=in_specs, out_specs=out_specs, check_vma=False
-    )
+        pick, mesh=mesh, in_specs=in_specs, out_specs=out_specs, check_vma=False
+    )

time: 370 us -> 153 us (0.41)
  waiting for transfers between devices: 215 us -> 0 us
  Pallas kernels: 0 us -> 144 us
  local copies, waits for them, and re-layouts: 47.7 us -> 7.82 us
  matrix products: 35.4 us -> 0 us
  other arithmetic: 31.6 us -> 0.68 us
  blocking collectives: 13.9 us -> 0 us
  between operations: 13.5 us -> 0.02 us
  starting transfers between devices: 11.1 us -> 0 us
    ppermute x3 -> x0, waiting for transfers between devices: 213 us -> none  [shifted(): return lax.ppermute(block, axis, route)]
    pallas_call x0 -> x1, Pallas kernels: none -> 144 us  [by_heads(): pl.pallas_call(functools.partial(heads_kernel, n), out_shape=jax.ShapeDty...]
    dot_general x12 -> x0, matrix products: 35.4 us -> none  [the longest x6 22.5 us: attend(): jnp.einsum('hqk,khd->qhd', weights.astype(jnp.bfloat16), value_rows, pref...]
    while x28 -> x0, local copies, waits for them, and re-layouts: 24.5 us -> none  [the longest x3 14.2 us: on_device(): lax.scan(one_group, running, (group_keys, group_values, group_mask))]
    reshape x4 -> x0, local copies, waits for them, and re-layouts: 13.9 us -> none  [the longest x1 6.87 us: on_device(): piece_keys.reshape(block_count // grouping, grouping * block_len, head_co...]
    all_gather x1 -> x0, blocking collectives: 13.9 us -> none  [on_device(): every_frame = lax.all_gather(frame_ids, 'seq', axis=0, tiled=True)]
    reduce_sum x6 -> x0, other arithmetic: 12.9 us -> none  [attend(): run_sum = run_sum * rescale + jnp.sum(weights, axis=-1)]
    ppermute x3 -> x0, starting transfers between devices: 11.1 us -> none  [shifted(): return lax.ppermute(block, axis, route)]
  transfers between devices with their start and end apart: 5 -> 0, of which waited for: 3 -> 0; matrix products, arithmetic and copies ran while one was open for 20% -> 0% of each run, Pallas kernels for 0% -> 0%
where the time goes in v1:
time: 153 us; the launch traced here: 152 us
  Pallas kernels  144 us (94%)
  local copies, waits for them, and re-layouts  7.82 us (5%)
    pallas_call x1, Pallas kernels, by_heads(): pl.pallas_call(functools.partial(heads_kernel, n), out_shape=jax.ShapeDty...  144 us
    unnamed x15, local copies, waits for them, and re-layouts  7.81 us

profile of v1, /device:TPU:0, one launch (start us, length us, event | category | flops | bytes accessed | tf_op | source)
XLA Modules:
  0.0 152.4 jit_solution(8305565510646741006)
XLA Ops:
  0.0 0.7 convert_element_type.4
  0.7 0.0 copy-start
  0.7 1.3 copy-done
  2.0 0.0 copy-start.1
  2.0 1.3 copy-done.1
  3.2 0.0 copy-start.2
  3.2 1.1 copy-done.2
  4.4 0.0 copy-start.3
  4.4 1.1 copy-done.3
  5.5 0.0 copy-start.4
  5.5 0.7 copy-done.4
  6.2 0.0 copy-start.5
  6.2 0.7 copy-done.5
  6.8 0.0 copy-start.6
  6.8 0.7 copy-done.6
  7.5 143.9 %shard_map.91 = bf16[384,1536]{1,0:T(8,128)(2,1)S(1)} custom-call(bf16[384,1536]{1,0:T(8,128)(2,1)S(1)} %copy-done, bf16[384,1536]{1,0:T(8,128)(2,1)S(1)} %copy-done.1, bf16[384,1536]{1,0:T(8,128)(2,1)} %v_ref.1, f32[8,384]{1,0:T(8,128)S(1)} %broadcast_in_dim.2.frames_ref, bf16[4,64,1536]{2,1,0:T(8,128)(2,1)S(1)} %copy-done.2, ...), custom_call_target="tpu_custom_call" | custom-call | tf_op jit(solution)/shard_map/pallas_call | solution.py:328
  151.4 1.0 copy.11
  (1 shorter events, 0.0 us)
Async XLA Ops:
  0.7 1.3 copy-start
  2.0 1.3 copy-start.1
  3.2 1.1 copy-start.2
  4.4 1.1 copy-start.3
  5.5 0.7 copy-start.4
  6.2 0.7 copy-start.5
  6.8 0.7 copy-start.6

commit v2 on v1

--- a/solution.py
+++ b/solution.py
@@ -122,7 +122,6 @@
 
 
 def heads_kernel(
-    n,
     q_ref,
     k_ref,
     v_ref,
@@ -142,17 +141,32 @@
     pvb,
     past_k,
     past_v,
+    part,
+    part_lse,
+    got,
+    got_lse,
+    own_acc,
+    own_stat,
     ob,
-    send_sem,
-    recv_sem,
+    q_send,
+    q_recv,
+    kv_send,
+    kv_recv,
     own_sem,
     frame_send,
     frame_recv,
+    part_send,
+    part_recv,
     out_send,
     out_recv,
     out_own,
 ):
+    n = 4
     me = lax.axis_index("seq")
+    side = lax.rem(me, 2)
+    half = me // 2
+    mate = me + 1 - 2 * side
+    peer = lax.rem(me + 2, n)
     rows = q_ref.shape[0]
     heads_here = qb.shape[0]
     width = heads_here * HEAD_DIM
@@ -168,48 +182,51 @@
         )
     pl.semaphore_wait(barrier, n - 1)
 
-    def pairs(h, dest, source):
-        columns = pl.ds(pl.multiple_of(dest * width + h * HEAD_DIM, HEAD_DIM), HEAD_DIM)
-        span = pl.ds(source * blocks, blocks)
+    def head_columns(which, h):
+        return pl.ds(pl.multiple_of(which * width + h * HEAD_DIM, HEAD_DIM), HEAD_DIM)
+
+    def remote(src, dst, send, recv, dest):
+        return pltpu.make_async_remote_copy(
+            src_ref=src,
+            dst_ref=dst,
+            send_sem=send,
+            recv_sem=recv,
+            device_id={"seq": dest},
+            device_id_type=MESH,
+        )
+
+    def stationary(h, which):
+        columns = head_columns(which, h)
+        span = pl.ds(side * blocks, blocks)
         return [
-            (q_ref.at[:, columns], qb.at[h, source]),
-            (k_ref.at[:, columns], kb.at[h, source]),
-            (v_ref.at[:, columns], vb.at[h, source]),
+            (k_ref.at[:, columns], kb.at[h, side]),
+            (v_ref.at[:, columns], vb.at[h, side]),
             (pk_ref.at[:, :, columns], pkb.at[h, span]),
             (pv_ref.at[:, :, columns], pvb.at[h, span]),
         ]
 
     def sends(h):
-        made = []
+        made = [
+            remote(src, dst, kv_send.at[h, i], kv_recv.at[h, i], mate)
+            for i, (src, dst) in enumerate(stationary(h, 1 - side))
+        ]
         for t in range(1, n):
             dest = lax.rem(me + t, n)
-            for i, (src, dst) in enumerate(pairs(h, dest, me)):
-                made.append(
-                    pltpu.make_async_remote_copy(
-                        src_ref=src,
-                        dst_ref=dst,
-                        send_sem=send_sem.at[h, t, i],
-                        recv_sem=recv_sem.at[h, t, i],
-                        device_id={"seq": dest},
-                        device_id_type=MESH,
-                    )
-                )
+            columns = head_columns(lax.rem(dest, 2), h)
+            made.append(
+                remote(q_ref.at[:, columns], qb.at[h, me], q_send.at[h, t], q_recv.at[h, t], dest)
+            )
         return made
 
     def owns(h):
+        mine = stationary(h, side) + [(q_ref.at[:, head_columns(side, h)], qb.at[h, me])]
         return [
-            pltpu.make_async_copy(src, dst, own_sem.at[h, i])
-            for i, (src, dst) in enumerate(pairs(h, me, me))
+            pltpu.make_async_copy(src, dst, own_sem.at[h, i]) for i, (src, dst) in enumerate(mine)
         ]
 
     def frame_send_of(t):
-        return pltpu.make_async_remote_copy(
-            src_ref=frames_ref,
-            dst_ref=fb.at[me],
-            send_sem=frame_send.at[t],
-            recv_sem=frame_recv.at[t],
-            device_id={"seq": lax.rem(me + t, n)},
-            device_id_type=MESH,
+        return remote(
+            frames_ref, fb.at[me], frame_send.at[t], frame_recv.at[t], lax.rem(me + t, n)
         )
 
     def start(h):
@@ -218,32 +235,87 @@
         for copy in owns(h):
             copy.start()
 
+    def part_copies(h):
+        return [
+            remote(part.at[h], got.at[h], part_send.at[h, 0], part_recv.at[h, 0], peer),
+            remote(part_lse.at[h], got_lse.at[h], part_send.at[h, 1], part_recv.at[h, 1], peer),
+        ]
+
+    def out_copy(h):
+        return remote(
+            ob.at[h, 1 - side],
+            out_ref.at[:, head_columns(side, h)],
+            out_send.at[h],
+            out_recv.at[h],
+            mate,
+        )
+
+    def out_own_copy(h):
+        return pltpu.make_async_copy(
+            ob.at[h, side], out_ref.at[:, head_columns(side, h)], out_own.at[h]
+        )
+
     for t in range(1, n):
         frame_send_of(t).start()
     start(0)
-    if heads_here > 1:
-        start(1)
+    start(1)
     fb[me] = frames_ref[...]
     for t in range(1, n):
         frame_send_of(t).wait()
     for s in range(n):
         frame_col[s] = jnp.transpose(fb[s])
 
-    def out_copy(h, t):
-        dest = lax.rem(me + t, n)
-        columns = pl.ds(pl.multiple_of(me * width + h * HEAD_DIM, HEAD_DIM), HEAD_DIM)
-        return pltpu.make_async_remote_copy(
-            src_ref=ob.at[h, dest],
-            dst_ref=out_ref.at[:, columns],
-            send_sem=out_send.at[h, t],
-            recv_sem=out_recv.at[h, t],
-            device_id={"seq": dest},
-            device_id_type=MESH,
-        )
-
-    def out_own_copy(h):
-        columns = pl.ds(pl.multiple_of(me * width + h * HEAD_DIM, HEAD_DIM), HEAD_DIM)
-        return pltpu.make_async_copy(ob.at[h, me], out_ref.at[:, columns], out_own.at[h])
+    def attend(h, g, s):
+        query = qb[h, s]
+        state = (
+            jnp.full((1, rows), -1e30, jnp.float32),
+            jnp.zeros((1, rows), jnp.float32),
+            jnp.zeros((HEAD_DIM, rows), jnp.float32),
+        )
+
+        def update(state, key, value, allowed):
+            top, total, acc = state
+            score = dot_nt(key, query) * scale
+            if allowed is not None:
+                score = jnp.where(allowed, score, -1e30)
+            new_top = jnp.maximum(top, jnp.max(score, axis=0, keepdims=True))
+            weight = jnp.exp2(score - new_top)
+            fade = jnp.exp2(top - new_top)
+            total = total * fade + jnp.sum(weight, axis=0, keepdims=True)
+            acc = acc * fade + dot_tn(value, weight.astype(jnp.bfloat16))
+            return new_top, total, acc
+
+        query_frame = fb[s, 0:1, :]
+        for i in range(2):
+            j = 2 * g + i
+            if j <= s + 1:
+                allowed = frame_col[j][:, 0:1] <= query_frame if j >= s else None
+                state = update(state, kb[h, i], vb[h, i], allowed)
+        keys, values = [], []
+        slot = lax.broadcasted_iota(jnp.int32, (win * blk, 1), 0) // blk
+        live = jnp.zeros((win * blk, 1), jnp.int32)
+        for w in range(win):
+            row = home_ref[windows_ref[s, w]]
+            keys.append(past_k[lax.rem(row, 2 * blocks)])
+            values.append(past_v[lax.rem(row, 2 * blocks)])
+            here = (row // (2 * blocks) == g) & (w < len_ref[s])
+            live = jnp.where(slot == w, here.astype(jnp.int32), live)
+        return update(
+            state, jnp.concatenate(keys, axis=0), jnp.concatenate(values, axis=0), live > 0
+        )
+
+    def merge(h):
+        for copy in part_copies(h):
+            copy.wait_recv()
+        for k in range(2):
+            top, total = own_stat[h, k, 0:1], own_stat[h, k, 1:2]
+            other = got_lse[h, k : k + 1]
+            new_top = jnp.maximum(top, other)
+            mine, theirs = jnp.exp2(top - new_top), jnp.exp2(other - new_top)
+            mixed = own_acc[h, k] * mine + got[h, k].astype(jnp.float32) * theirs
+            ob[h, k] = jnp.transpose(mixed / (total * mine + theirs)).astype(jnp.bfloat16)
+        out_copy(h).start()
+        out_own_copy(h).start()
 
     def one_head(h, carry):
         for copy in sends(h):
@@ -257,55 +329,42 @@
 
         past_k[...] = pkb[h]
         past_v[...] = pvb[h]
-        for s in range(n):
-            query = qb[h, s]
-            state = (
-                jnp.full((1, rows), -1e30, jnp.float32),
-                jnp.zeros((1, rows), jnp.float32),
-                jnp.zeros((HEAD_DIM, rows), jnp.float32),
-            )
-
-            def update(state, key, value, allowed):
-                top, total, acc = state
-                score = dot_nt(key, query) * scale
-                if allowed is not None:
-                    score = jnp.where(allowed, score, -1e30)
-                new_top = jnp.maximum(top, jnp.max(score, axis=0, keepdims=True))
-                weight = jnp.exp2(score - new_top)
-                fade = jnp.exp2(top - new_top)
-                total = total * fade + jnp.sum(weight, axis=0, keepdims=True)
-                acc = acc * fade + dot_tn(value, weight.astype(jnp.bfloat16))
-                return new_top, total, acc
-
-            query_frame = fb[s, 0:1, :]
-            for j in range(min(s + 2, n)):
-                allowed = None
-                if j >= s:
-                    allowed = frame_col[j][:, 0:1] <= query_frame
-                state = update(state, kb[h, j], vb[h, j], allowed)
-            keys, values, live = [], [], []
-            for w in range(win):
-                row = home_ref[windows_ref[s, w]]
-                keys.append(past_k[row])
-                values.append(past_v[row])
-            slot = lax.broadcasted_iota(jnp.int32, (win * blk, 1), 0) // blk
-            live = slot < len_ref[s]
-            top, total, acc = update(
-                state, jnp.concatenate(keys, axis=0), jnp.concatenate(values, axis=0), live
-            )
-            ob[h, s] = jnp.transpose(acc / total).astype(jnp.bfloat16)
-        for t in range(1, n):
-            out_copy(h, t).start()
-        out_own_copy(h).start()
+
+        def away(g):
+            for k in range(2):
+                top, total, acc = attend(h, g, 2 * (1 - g) + k)
+                part[h, k] = (acc / total).astype(jnp.bfloat16)
+                part_lse[h, k : k + 1] = top + jnp.log2(total)
+
+        def home(g):
+            for k in range(2):
+                top, total, acc = attend(h, g, 2 * g + k)
+                own_acc[h, k] = acc
+                own_stat[h, k, 0:1] = top
+                own_stat[h, k, 1:2] = total
+
+        for g in range(2):
+            pl.when(half == g)(functools.partial(away, g))
+        for copy in part_copies(h):
+            copy.start()
+        for g in range(2):
+            pl.when(half == g)(functools.partial(home, g))
+
+        @pl.when(h > 0)
+        def _():
+            merge(h - 1)
+
         return carry
 
     lax.fori_loop(0, heads_here, one_head, 0)
+    merge(heads_here - 1)
 
     def finish(h, carry):
         for copy in sends(h):
             copy.wait_send()
-        for t in range(1, n):
-            out_copy(h, t).wait()
+        for copy in part_copies(h):
+            copy.wait_send()
+        out_copy(h).wait()
         out_own_copy(h).wait()
         return carry
 
@@ -317,37 +376,47 @@
 ):
     n = lax.axis_size("seq")
     rows, features = queries.shape
-    heads_here = features // HEAD_DIM // n
+    heads_here = features // HEAD_DIM // 2
     blocks, blk = past_keys.shape[0], past_keys.shape[1]
     frames = jnp.broadcast_to(frame_ids[None, :].astype(jnp.float32), (8, rows))
     anywhere = pl.BlockSpec(memory_space=pl.ANY)
     vmem = pl.BlockSpec(memory_space=pltpu.VMEM)
     smem = pl.BlockSpec(memory_space=pltpu.SMEM)
     dma = pltpu.SemaphoreType.DMA
-    bf16 = jnp.bfloat16
+    bf16, f32 = jnp.bfloat16, jnp.float32
     return pl.pallas_call(
-        functools.partial(heads_kernel, n),
+        heads_kernel,
         out_shape=jax.ShapeDtypeStruct((rows, features), bf16),
         in_specs=[anywhere] * 3 + [vmem] + [anywhere] * 2 + [smem] * 3,
         out_specs=anywhere,
         scratch_shapes=[
             pltpu.VMEM((heads_here, n, rows, HEAD_DIM), bf16),
-            pltpu.VMEM((heads_here, n, rows, HEAD_DIM), bf16),
-            pltpu.VMEM((heads_here, n, rows, HEAD_DIM), bf16),
-            pltpu.VMEM((n, 8, rows), jnp.float32),
-            pltpu.VMEM((n, rows, 8), jnp.float32),
-            pltpu.VMEM((heads_here, n * blocks, blk, HEAD_DIM), bf16),
-            pltpu.VMEM((heads_here, n * blocks, blk, HEAD_DIM), bf16),
-            pltpu.VMEM((n * blocks, blk, HEAD_DIM), bf16),
-            pltpu.VMEM((n * blocks, blk, HEAD_DIM), bf16),
-            pltpu.VMEM((heads_here, n, rows, HEAD_DIM), bf16),
-            dma((heads_here, n, 5)),
-            dma((heads_here, n, 5)),
+            pltpu.VMEM((heads_here, 2, rows, HEAD_DIM), bf16),
+            pltpu.VMEM((heads_here, 2, rows, HEAD_DIM), bf16),
+            pltpu.VMEM((n, 8, rows), f32),
+            pltpu.VMEM((n, rows, 8), f32),
+            pltpu.VMEM((heads_here, 2 * blocks, blk, HEAD_DIM), bf16),
+            pltpu.VMEM((heads_here, 2 * blocks, blk, HEAD_DIM), bf16),
+            pltpu.VMEM((2 * blocks, blk, HEAD_DIM), bf16),
+            pltpu.VMEM((2 * blocks, blk, HEAD_DIM), bf16),
+            pltpu.VMEM((heads_here, 2, HEAD_DIM, rows), bf16),
+            pltpu.VMEM((heads_here, 2, rows), f32),
+            pltpu.VMEM((heads_here, 2, HEAD_DIM, rows), bf16),
+            pltpu.VMEM((heads_here, 2, rows), f32),
+            pltpu.VMEM((heads_here, 2, HEAD_DIM, rows), f32),
+            pltpu.VMEM((heads_here, 2, 2, rows), f32),
+            pltpu.VMEM((heads_here, 2, rows, HEAD_DIM), bf16),
+            dma((heads_here, n)),
+            dma((heads_here, n)),
+            dma((heads_here, 4)),
+            dma((heads_here, 4)),
             dma((heads_here, 5)),
             dma((n,)),
             dma((n,)),
-            dma((heads_here, n)),
-            dma((heads_here, n)),
+            dma((heads_here, 2)),
+            dma((heads_here, 2)),
+            dma((heads_here,)),
+            dma((heads_here,)),
             dma((heads_here,)),
         ],
         compiler_params=pltpu.CompilerParams(
@@ -358,7 +427,7 @@
 
 def pick(queries, *rest):
     heads = queries.shape[1] // HEAD_DIM
-    if heads % lax.axis_size("seq") == 0:
+    if lax.axis_size("seq") == 4 and heads % 2 == 0 and heads >= 4:
         return by_heads(queries, *rest)
     return on_device(queries, *rest)
 

time: 153 us -> 137 us (0.90)
  Pallas kernels: 144 us -> 128 us
    pallas_call x1, Pallas kernels: 144 us -> 128 us  [by_heads(): pl.pallas_call(heads_kernel, out_shape=jax.ShapeDtypeStruct((rows, featur...]
where the time goes in v2:
time: 137 us; the launch traced here: 136 us
  Pallas kernels  128 us (93%)
  local copies, waits for them, and re-layouts  7.82 us (6%)
    pallas_call x1, Pallas kernels, by_heads(): pl.pallas_call(heads_kernel, out_shape=jax.ShapeDtypeStruct((rows, featur...  128 us
    unnamed x15, local copies, waits for them, and re-layouts  7.81 us

profile of v2, /device:TPU:0, one launch (start us, length us, event | category | flops | bytes accessed | tf_op | source)
XLA Modules:
  0.0 136.4 jit_solution(3484295034129273533)
XLA Ops:
  0.0 0.7 convert_element_type.4
  0.7 0.0 copy-start
  0.7 1.3 copy-done
  2.0 0.0 copy-start.1
  2.0 1.3 copy-done.1
  3.2 0.0 copy-start.2
  3.2 1.1 copy-done.2
  4.4 0.0 copy-start.3
  4.4 1.1 copy-done.3
  5.5 0.0 copy-start.4
  5.5 0.7 copy-done.4
  6.2 0.0 copy-start.5
  6.2 0.7 copy-done.5
  6.8 0.0 copy-start.6
  6.8 0.7 copy-done.6
  7.5 127.9 %shard_map.91 = bf16[384,1536]{1,0:T(8,128)(2,1)S(1)} custom-call(bf16[384,1536]{1,0:T(8,128)(2,1)S(1)} %copy-done, bf16[384,1536]{1,0:T(8,128)(2,1)S(1)} %copy-done.1, bf16[384,1536]{1,0:T(8,128)(2,1)} %v_ref.1, f32[8,384]{1,0:T(8,128)S(1)} %broadcast_in_dim.2.frames_ref, bf16[4,64,1536]{2,1,0:T(8,128)(2,1)S(1)} %copy-done.2, ...), custom_call_target="tpu_custom_call" | custom-call | tf_op jit(solution)/shard_map/pallas_call | solution.py:387
  135.4 1.0 copy.11
  (1 shorter events, 0.0 us)
Async XLA Ops:
  0.7 1.3 copy-start
  2.0 1.3 copy-start.1
  3.2 1.1 copy-start.2
  4.4 1.1 copy-start.3
  5.5 0.7 copy-start.4
  6.2 0.7 copy-start.5
  6.8 0.7 copy-start.6

commit v3 on v2

--- a/solution.py
+++ b/solution.py
@@ -145,11 +145,15 @@
     part_lse,
     got,
     got_lse,
+    met,
+    met_lse,
     own_acc,
     own_stat,
     ob,
+    ob_met,
     q_send,
     q_recv,
+    relay_send,
     kv_send,
     kv_recv,
     own_sem,
@@ -160,6 +164,7 @@
     out_send,
     out_recv,
     out_own,
+    out_met,
 ):
     n = 4
     me = lax.axis_index("seq")
@@ -167,6 +172,8 @@
     half = me // 2
     mate = me + 1 - 2 * side
     peer = lax.rem(me + 2, n)
+    outer = side == half
+    inner = side != half
     rows = q_ref.shape[0]
     heads_here = qb.shape[0]
     width = heads_here * HEAD_DIM
@@ -205,18 +212,33 @@
             (pv_ref.at[:, :, columns], pvb.at[h, span]),
         ]
 
-    def sends(h):
-        made = [
+    def kv_sends(h):
+        return [
             remote(src, dst, kv_send.at[h, i], kv_recv.at[h, i], mate)
             for i, (src, dst) in enumerate(stationary(h, 1 - side))
         ]
-        for t in range(1, n):
-            dest = lax.rem(me + t, n)
-            columns = head_columns(lax.rem(dest, 2), h)
-            made.append(
-                remote(q_ref.at[:, columns], qb.at[h, me], q_send.at[h, t], q_recv.at[h, t], dest)
-            )
-        return made
+
+    def q_copy(h, t):
+        dest = lax.rem(me + t, n)
+        columns = head_columns(lax.rem(dest, 2), h)
+        return remote(q_ref.at[:, columns], qb.at[h, me], q_send.at[h, t], q_recv.at[h, t], dest)
+
+    def direct(t):
+        return jnp.logical_or(inner, lax.rem(me + t, n) != n - 1 - me)
+
+    def unrelayed(t):
+        return jnp.logical_or(outer, lax.rem(me - t + n, n) != mate)
+
+    def relay_copy(h):
+        dest = n - 1 - mate
+        t = lax.rem(dest - mate + n, n)
+        return remote(qb.at[h, mate], qb.at[h, mate], relay_send.at[h], q_recv.at[h, t], dest)
+
+    def relay(h):
+        @pl.when(inner)
+        def _():
+            q_copy(h, lax.rem(me - mate + n, n)).wait_recv()
+            relay_copy(h).start()
 
     def owns(h):
         mine = stationary(h, side) + [(q_ref.at[:, head_columns(side, h)], qb.at[h, me])]
@@ -230,16 +252,30 @@
         )
 
     def start(h):
-        for copy in sends(h):
+        for t in (1, 3, 2):
+            pl.when(direct(t))(q_copy(h, t).start)
+        for copy in kv_sends(h):
             copy.start()
         for copy in owns(h):
             copy.start()
 
-    def part_copies(h):
+    def both(h, i, src, dst, dst_lse, where, dest):
         return [
-            remote(part.at[h], got.at[h], part_send.at[h, 0], part_recv.at[h, 0], peer),
-            remote(part_lse.at[h], got_lse.at[h], part_send.at[h, 1], part_recv.at[h, 1], peer),
+            remote(part.at[h, src], dst.at[h, where], part_send.at[h, i, 0], part_recv.at[h, i, 0], dest),
+            remote(part_lse.at[h, src], dst_lse.at[h, where], part_send.at[h, i, 1], part_recv.at[h, i, 1], dest),
         ]
+
+    def far_outer(h):
+        return both(h, 0, 1 - half, got, got_lse, 1 - half, peer)
+
+    def far_inner_by_outer(h):
+        return both(h, 1, half, got, got_lse, half, peer)
+
+    def far_inner_by_inner(h):
+        return both(h, 2, half, met, met_lse, 1, n - 1 - me)
+
+    def near_inner_by_outer(h):
+        return both(h, 3, 2, met, met_lse, 0, mate)
 
     def out_copy(h):
         return remote(
@@ -255,15 +291,22 @@
             ob.at[h, side], out_ref.at[:, head_columns(side, h)], out_own.at[h]
         )
 
+    def out_met_copy(h):
+        return pltpu.make_async_copy(
+            ob_met.at[h], out_ref.at[:, head_columns(1 - side, h)], out_met.at[h]
+        )
+
     for t in range(1, n):
         frame_send_of(t).start()
     start(0)
     start(1)
+    start(2)
     fb[me] = frames_ref[...]
     for t in range(1, n):
         frame_send_of(t).wait()
     for s in range(n):
         frame_col[s] = jnp.transpose(fb[s])
+    relay(0)
 
     def attend(h, g, s):
         query = qb[h, s]
@@ -304,28 +347,53 @@
             state, jnp.concatenate(keys, axis=0), jnp.concatenate(values, axis=0), live > 0
         )
 
+    def merge_own(h, k):
+        top, total = own_stat[h, k, 0:1], own_stat[h, k, 1:2]
+        other = got_lse[h, k]
+        new_top = jnp.maximum(top, other)
+        mine, theirs = jnp.exp2(top - new_top), jnp.exp2(other - new_top)
+        mixed = own_acc[h, k] * mine + got[h, k].astype(jnp.float32) * theirs
+        ob[h, k] = jnp.transpose(mixed / (total * mine + theirs)).astype(jnp.bfloat16)
+
+    def merge_met(h):
+        one, two = met_lse[h, 0], met_lse[h, 1]
+        top = jnp.maximum(one, two)
+        one, two = jnp.exp2(one - top), jnp.exp2(two - top)
+        mixed = met[h, 0].astype(jnp.float32) * one + met[h, 1].astype(jnp.float32) * two
+        ob_met[h] = jnp.transpose(mixed / (one + two)).astype(jnp.bfloat16)
+
     def merge(h):
-        for copy in part_copies(h):
+        for copy in both(h, 0, 0, got, got_lse, half, peer):
             copy.wait_recv()
-        for k in range(2):
-            top, total = own_stat[h, k, 0:1], own_stat[h, k, 1:2]
-            other = got_lse[h, k : k + 1]
-            new_top = jnp.maximum(top, other)
-            mine, theirs = jnp.exp2(top - new_top), jnp.exp2(other - new_top)
-            mixed = own_acc[h, k] * mine + got[h, k].astype(jnp.float32) * theirs
-            ob[h, k] = jnp.transpose(mixed / (total * mine + theirs)).astype(jnp.bfloat16)
-        out_copy(h).start()
-        out_own_copy(h).start()
+        merge_own(h, half)
+
+        @pl.when(outer)
+        def _():
+            out_own_copy(h).start()
+
+        @pl.when(inner)
+        def _():
+            out_copy(h).start()
+            for copy in both(h, 1, 0, got, got_lse, 1 - half, peer):
+                copy.wait_recv()
+            merge_own(h, 1 - half)
+            out_own_copy(h).start()
+            for copy in far_inner_by_inner(h) + near_inner_by_outer(h):
+                copy.wait_recv()
+            merge_met(h)
+            out_met_copy(h).start()
 
     def one_head(h, carry):
-        for copy in sends(h):
+        for t in range(1, n):
+            pl.when(unrelayed(t))(q_copy(h, t).wait_recv)
+        for copy in kv_sends(h):
             copy.wait_recv()
         for copy in owns(h):
             copy.wait()
 
-        @pl.when(h + 2 < heads_here)
-        def _():
-            start(h + 2)
+        @pl.when(h + 3 < heads_here)
+        def _():
+            start(h + 3)
 
         past_k[...] = pkb[h]
         past_v[...] = pvb[h]
@@ -334,7 +402,7 @@
             for k in range(2):
                 top, total, acc = attend(h, g, 2 * (1 - g) + k)
                 part[h, k] = (acc / total).astype(jnp.bfloat16)
-                part_lse[h, k : k + 1] = top + jnp.log2(total)
+                part_lse[h, k] = top + jnp.log2(total)
 
         def home(g):
             for k in range(2):
@@ -342,14 +410,37 @@
                 own_acc[h, k] = acc
                 own_stat[h, k, 0:1] = top
                 own_stat[h, k, 1:2] = total
+                if k != g:
+                    part[h, 2] = (acc / total).astype(jnp.bfloat16)
+                    part_lse[h, 2] = top + jnp.log2(total)
 
         for g in range(2):
             pl.when(half == g)(functools.partial(away, g))
-        for copy in part_copies(h):
+        for copy in far_outer(h):
             copy.start()
+
+        @pl.when(outer)
+        def _():
+            for copy in far_inner_by_outer(h):
+                copy.start()
+
+        @pl.when(inner)
+        def _():
+            for copy in far_inner_by_inner(h):
+                copy.start()
+
+        @pl.when(h + 1 < heads_here)
+        def _():
+            relay(h + 1)
+
         for g in range(2):
             pl.when(half == g)(functools.partial(home, g))
 
+        @pl.when(outer)
+        def _():
+            for copy in near_inner_by_outer(h):
+                copy.start()
+
         @pl.when(h > 0)
         def _():
             merge(h - 1)
@@ -360,12 +451,26 @@
     merge(heads_here - 1)
 
     def finish(h, carry):
-        for copy in sends(h):
+        for t in range(1, n):
+            pl.when(direct(t))(q_copy(h, t).wait_send)
+        for copy in kv_sends(h) + far_outer(h):
             copy.wait_send()
-        for copy in part_copies(h):
-            copy.wait_send()
-        out_copy(h).wait()
         out_own_copy(h).wait()
+
+        @pl.when(outer)
+        def _():
+            for copy in far_inner_by_outer(h) + near_inner_by_outer(h):
+                copy.wait_send()
+            out_copy(h).wait_recv()
+
+        @pl.when(inner)
+        def _():
+            relay_copy(h).wait_send()
+            for copy in far_inner_by_inner(h):
+                copy.wait_send()
+            out_copy(h).wait_send()
+            out_met_copy(h).wait()
+
         return carry
 
     lax.fori_loop(0, heads_here, finish, 0)
@@ -399,22 +504,27 @@
             pltpu.VMEM((heads_here, 2 * blocks, blk, HEAD_DIM), bf16),
             pltpu.VMEM((2 * blocks, blk, HEAD_DIM), bf16),
             pltpu.VMEM((2 * blocks, blk, HEAD_DIM), bf16),
+            pltpu.VMEM((heads_here, 3, HEAD_DIM, rows), bf16),
+            pltpu.VMEM((heads_here, 3, 1, rows), f32),
             pltpu.VMEM((heads_here, 2, HEAD_DIM, rows), bf16),
-            pltpu.VMEM((heads_here, 2, rows), f32),
+            pltpu.VMEM((heads_here, 2, 1, rows), f32),
             pltpu.VMEM((heads_here, 2, HEAD_DIM, rows), bf16),
-            pltpu.VMEM((heads_here, 2, rows), f32),
+            pltpu.VMEM((heads_here, 2, 1, rows), f32),
             pltpu.VMEM((heads_here, 2, HEAD_DIM, rows), f32),
             pltpu.VMEM((heads_here, 2, 2, rows), f32),
             pltpu.VMEM((heads_here, 2, rows, HEAD_DIM), bf16),
+            pltpu.VMEM((heads_here, rows, HEAD_DIM), bf16),
             dma((heads_here, n)),
             dma((heads_here, n)),
+            dma((heads_here,)),
             dma((heads_here, 4)),
             dma((heads_here, 4)),
             dma((heads_here, 5)),
             dma((n,)),
             dma((n,)),
-            dma((heads_here, 2)),
-            dma((heads_here, 2)),
+            dma((heads_here, 4, 2)),
+            dma((heads_here, 4, 2)),
+            dma((heads_here,)),
             dma((heads_here,)),
             dma((heads_here,)),
             dma((heads_here,)),
@@ -427,7 +537,7 @@
 
 def pick(queries, *rest):
     heads = queries.shape[1] // HEAD_DIM
-    if lax.axis_size("seq") == 4 and heads % 2 == 0 and heads >= 4:
+    if lax.axis_size("seq") == 4 and heads % 2 == 0 and heads >= 6:
         return by_heads(queries, *rest)
     return on_device(queries, *rest)
 

time: 137 us -> 132 us (0.964)
  Pallas kernels: 128 us -> 123 us
    pallas_call x1, Pallas kernels: 128 us -> 123 us  [by_heads(): pl.pallas_call(heads_kernel, out_shape=jax.ShapeDtypeStruct((rows, featur...]
where the time goes in v3:
time: 132 us; the launch traced here: 131 us
  Pallas kernels  123 us (93%)
  local copies, waits for them, and re-layouts  7.82 us (6%)
    pallas_call x1, Pallas kernels, by_heads(): pl.pallas_call(heads_kernel, out_shape=jax.ShapeDtypeStruct((rows, featur...  123 us
    unnamed x15, local copies, waits for them, and re-layouts  7.81 us

profile of v3, /device:TPU:0, one launch (start us, length us, event | category | flops | bytes accessed | tf_op | source)
XLA Modules:
  0.0 131.5 jit_solution(15588061987979570781)
XLA Ops:
  0.0 0.7 convert_element_type.4
  0.7 0.0 copy-start
  0.7 1.3 copy-done
  2.0 0.0 copy-start.1
  2.0 1.3 copy-done.1
  3.2 0.0 copy-start.2
  3.2 1.1 copy-done.2
  4.4 0.0 copy-start.3
  4.4 1.1 copy-done.3
  5.5 0.0 copy-start.4
  5.5 0.7 copy-done.4
  6.2 0.0 copy-start.5
  6.2 0.7 copy-done.5
  6.8 0.0 copy-start.6
  6.8 0.7 copy-done.6
  7.5 123.0 %shard_map.91 = bf16[384,1536]{1,0:T(8,128)(2,1)S(1)} custom-call(bf16[384,1536]{1,0:T(8,128)(2,1)S(1)} %copy-done, bf16[384,1536]{1,0:T(8,128)(2,1)S(1)} %copy-done.1, bf16[384,1536]{1,0:T(8,128)(2,1)} %v_ref.1, f32[8,384]{1,0:T(8,128)S(1)} %broadcast_in_dim.2.frames_ref, bf16[4,64,1536]{2,1,0:T(8,128)(2,1)S(1)} %copy-done.2, ...), custom_call_target="tpu_custom_call" | custom-call | tf_op jit(solution)/shard_map/pallas_call | solution.py:492
  130.5 1.0 copy.11
  (1 shorter events, 0.0 us)
Async XLA Ops:
  0.7 1.3 copy-start
  2.0 1.3 copy-start.1
  3.2 1.1 copy-start.2
  4.4 1.1 copy-start.3
  5.5 0.7 copy-start.4
  6.2 0.7 copy-start.5
  6.8 0.7 copy-start.6

commit v4 on v3

--- a/solution.py
+++ b/solution.py
@@ -300,7 +300,6 @@
         frame_send_of(t).start()
     start(0)
     start(1)
-    start(2)
     fb[me] = frames_ref[...]
     for t in range(1, n):
         frame_send_of(t).wait()
@@ -391,9 +390,9 @@
         for copy in owns(h):
             copy.wait()
 
-        @pl.when(h + 3 < heads_here)
-        def _():
-            start(h + 3)
+        @pl.when(h + 2 < heads_here)
+        def _():
+            start(h + 2)
 
         past_k[...] = pkb[h]
         past_v[...] = pvb[h]

time: 132 us -> 125 us (0.947)
  Pallas kernels: 123 us -> 116 us
    pallas_call x1, Pallas kernels: 123 us -> 116 us  [by_heads(): pl.pallas_call(heads_kernel, out_shape=jax.ShapeDtypeStruct((rows, featur...]
where the time goes in v4:
time: 125 us; the launch traced here: 124 us
  Pallas kernels  116 us (93%)
  local copies, waits for them, and re-layouts  7.82 us (6%)
    pallas_call x1, Pallas kernels, by_heads(): pl.pallas_call(heads_kernel, out_shape=jax.ShapeDtypeStruct((rows, featur...  116 us
    unnamed x15, local copies, waits for them, and re-layouts  7.81 us

profile of v4, /device:TPU:0, one launch (start us, length us, event | category | flops | bytes accessed | tf_op | source)
XLA Modules:
  0.0 124.3 jit_solution(5020962360087166256)
XLA Ops:
  0.0 0.7 convert_element_type.4
  0.7 0.0 copy-start
  0.7 1.3 %copy-done = bf16[384,1536]{1,0:T(8,128)(2,1)S(1)} copy-done((bf16[384,1536]{1,0:T(8,128)(2,1)S(1)}, bf16[384,1536]{1,0:T(8,128)(2,1)}, u32[]{:S(2)}) %copy-start) | copy-done | bytes 1179672
  2.0 0.0 copy-start.1
  2.0 1.3 %copy-done.1 = bf16[384,1536]{1,0:T(8,128)(2,1)S(1)} copy-done((bf16[384,1536]{1,0:T(8,128)(2,1)S(1)}, bf16[384,1536]{1,0:T(8,128)(2,1)}, u32[]{:S(2)}) %copy-start.1) | copy-done | bytes 1179672
  3.2 0.0 copy-start.2
  3.2 1.1 copy-done.2
  4.4 0.0 copy-start.3
  4.4 1.1 copy-done.3
  5.5 0.0 copy-start.4
  5.5 0.7 copy-done.4
  6.2 0.0 copy-start.5
  6.2 0.7 copy-done.5
  6.8 0.0 copy-start.6
  6.8 0.7 copy-done.6
  7.5 115.8 %shard_map.91 = bf16[384,1536]{1,0:T(8,128)(2,1)S(1)} custom-call(bf16[384,1536]{1,0:T(8,128)(2,1)S(1)} %copy-done, bf16[384,1536]{1,0:T(8,128)(2,1)S(1)} %copy-done.1, bf16[384,1536]{1,0:T(8,128)(2,1)} %v_ref.1, f32[8,384]{1,0:T(8,128)S(1)} %broadcast_in_dim.2.frames_ref, bf16[4,64,1536]{2,1,0:T(8,128)(2,1)S(1)} %copy-done.2, ...), custom_call_target="tpu_custom_call" | custom-call | tf_op jit(solution)/shard_map/pallas_call | solution.py:491
  123.3 1.0 copy.11
  (1 shorter events, 0.0 us)
Async XLA Ops:
  0.7 1.3 %copy-start = (bf16[384,1536]{1,0:T(8,128)(2,1)S(1)}, bf16[384,1536]{1,0:T(8,128)(2,1)}, u32[]{:S(2)}) copy-start(bf16[384,1536]{1,0:T(8,128)(2,1)} %q_ref.1) | copy-start | bytes 3538948
  2.0 1.3 %copy-start.1 = (bf16[384,1536]{1,0:T(8,128)(2,1)S(1)}, bf16[384,1536]{1,0:T(8,128)(2,1)}, u32[]{:S(2)}) copy-start(bf16[384,1536]{1,0:T(8,128)(2,1)} %k_ref.1) | copy-start | bytes 3538948
  3.2 1.1 copy-start.2
  4.4 1.1 copy-start.3
  5.5 0.7 copy-start.4
  6.2 0.7 copy-start.5
  6.8 0.7 copy-start.6

commit v5 on v4

--- a/solution.py
+++ b/solution.py
@@ -390,10 +390,6 @@
         for copy in owns(h):
             copy.wait()
 
-        @pl.when(h + 2 < heads_here)
-        def _():
-            start(h + 2)
-
         past_k[...] = pkb[h]
         past_v[...] = pvb[h]
 
@@ -431,6 +427,10 @@
         @pl.when(h + 1 < heads_here)
         def _():
             relay(h + 1)
+
+        @pl.when(h + 2 < heads_here)
+        def _():
+            start(h + 2)
 
         for g in range(2):
             pl.when(half == g)(functools.partial(home, g))

time: 125 us -> 125 us (level)
  no operation moved by 1% of the time
where the time goes in v5:
time: 125 us; the launch traced here: 124 us
  Pallas kernels  116 us (93%)
  local copies, waits for them, and re-layouts  7.82 us (6%)
    pallas_call x1, Pallas kernels, by_heads(): pl.pallas_call(heads_kernel, out_shape=jax.ShapeDtypeStruct((rows, featur...  116 us
    unnamed x15, local copies, waits for them, and re-layouts  7.81 us

profile of v5, /device:TPU:0, one launch (start us, length us, event | category | flops | bytes accessed | tf_op | source)
XLA Modules:
  0.0 124.4 jit_solution(4412192277795697525)
XLA Ops:
  0.0 0.7 convert_element_type.4
  0.7 0.0 copy-start
  0.7 1.3 %copy-done = bf16[384,1536]{1,0:T(8,128)(2,1)S(1)} copy-done((bf16[384,1536]{1,0:T(8,128)(2,1)S(1)}, bf16[384,1536]{1,0:T(8,128)(2,1)}, u32[]{:S(2)}) %copy-start) | copy-done | bytes 1179672
  2.0 0.0 copy-start.1
  2.0 1.3 %copy-done.1 = bf16[384,1536]{1,0:T(8,128)(2,1)S(1)} copy-done((bf16[384,1536]{1,0:T(8,128)(2,1)S(1)}, bf16[384,1536]{1,0:T(8,128)(2,1)}, u32[]{:S(2)}) %copy-start.1) | copy-done | bytes 1179672
  3.2 0.0 copy-start.2
  3.2 1.1 copy-done.2
  4.4 0.0 copy-start.3
  4.4 1.1 copy-done.3
  5.5 0.0 copy-start.4
  5.5 0.7 copy-done.4
  6.2 0.0 copy-start.5
  6.2 0.7 copy-done.5
  6.8 0.0 copy-start.6
  6.8 0.7 copy-done.6
  7.5 115.9 %shard_map.91 = bf16[384,1536]{1,0:T(8,128)(2,1)S(1)} custom-call(bf16[384,1536]{1,0:T(8,128)(2,1)S(1)} %copy-done, bf16[384,1536]{1,0:T(8,128)(2,1)S(1)} %copy-done.1, bf16[384,1536]{1,0:T(8,128)(2,1)} %v_ref.1, f32[8,384]{1,0:T(8,128)S(1)} %broadcast_in_dim.2.frames_ref, bf16[4,64,1536]{2,1,0:T(8,128)(2,1)S(1)} %copy-done.2, ...), custom_call_target="tpu_custom_call" | custom-call | tf_op jit(solution)/shard_map/pallas_call | solution.py:491
  123.4 1.0 copy.11
  (1 shorter events, 0.0 us)
Async XLA Ops:
  0.7 1.3 %copy-start = (bf16[384,1536]{1,0:T(8,128)(2,1)S(1)}, bf16[384,1536]{1,0:T(8,128)(2,1)}, u32[]{:S(2)}) copy-start(bf16[384,1536]{1,0:T(8,128)(2,1)} %q_ref.1) | copy-start | bytes 3538948
  2.0 1.3 %copy-start.1 = (bf16[384,1536]{1,0:T(8,128)(2,1)S(1)}, bf16[384,1536]{1,0:T(8,128)(2,1)}, u32[]{:S(2)}) copy-start(bf16[384,1536]{1,0:T(8,128)(2,1)} %k_ref.1) | copy-start | bytes 3538948
  3.2 1.1 copy-start.2
  4.4 1.1 copy-start.3
  5.5 0.7 copy-start.4
  6.2 0.7 copy-start.5
  6.8 0.7 copy-start.6
